TPU v7x, 512 devices: a whole 4x8x8 slice. The times are simulated.
512 devices in a mesh: dp: 16 (over z_lo, x), zero: 32 (over y, z_hi, core).
Axes of the slice: x: 4, y: 8, z: 8 (z_hi: 2, z_lo: 4; z = z_hi * 4 + z_lo), core: 2. Of those that a mesh axis runs over, the one named last changes fastest.
Arguments:
- gate_up: bfloat16 [2, 4096, 14336], P(None, 'dp', 'zero'), may hold values from -6 to 6
- cot_mean: bfloat16 [4096, 4096], P('dp', 'zero'), may hold values from -6 to 6
- label_rows: bfloat16 [64, 4096], P(None, 'dp'), may hold values from -6 to 6
- true_labels: int32 [4096], P('dp'), may hold values from 0 to 63
- sampled_labels: int32 [4096], P('dp'), may hold values from 0 to 63
- weight: bfloat16 [14336, 4096], P('zero', 'dp'), may hold values from -4 to 4
- moment: bfloat16 [14336, 4096], P('zero', 'dp'), may hold values from -0.29882812 to 0.29882812
- curvature: bfloat16 [14336, 4096], P('zero', 'dp'), may hold values from 0.0099487305 to 1
- bits: int32 [14336, 4096], P('zero', 'dp'), may hold values from 0 to 16383
Outputs:
- new_weight: bfloat16 [14336, 4096], P('zero')
- new_moment: bfloat16 [14336, 4096], P('zero', 'dp')
- new_curvature: bfloat16 [14336, 4096], P('zero', 'dp')
All inputs are finite; a program needn't handle non-finite values.
Results may differ from a plain program's by a relative error of at most 0.014.
Values may be sent and summed in bfloat16 or wider, within the bound.
A program may use at most 64 MiB of HBM per device.

v0:
```python
import math
import jax
import jax.numpy as jnp
from jax import lax
from jax.sharding import PartitionSpec as P

beta_one = 0.965
beta_two = 0.99
gamma_rate = 0.5
learn_rate = 0.05
decay_rate = 0.1


def dither(value, noise):
    return (value * (1.0 + (noise - 0.5) / 8.0)).astype(jnp.bfloat16)


def on_device(
    gate_up, cot_mean, label_rows, true_labels, sampled_labels, weight, moment, curvature, bits
):
    tok_rows = gate_up.shape[1]
    cands = label_rows.shape[0]
    groups = lax.axis_size("dp")
    factor = 1.0 / math.sqrt(tok_rows * groups)
    gate_part = gate_up[0].astype(jnp.float32)
    up_part = gate_up[1].astype(jnp.float32)
    hidden = (jax.nn.silu(gate_part) * up_part).astype(jnp.bfloat16)
    classes = jnp.arange(cands, dtype=jnp.int32)
    hot_true = (true_labels[:, None] == classes[None, :]).astype(jnp.bfloat16)
    hot_sampled = (sampled_labels[:, None] == classes[None, :]).astype(jnp.bfloat16)
    label_part = jnp.dot(
        hidden.T,
        jnp.concatenate([hot_true, hot_sampled], axis=1),
        preferred_element_type=jnp.float32,
    )
    label_total = lax.psum(label_part.astype(jnp.bfloat16), "dp").astype(jnp.float32)
    terms = jnp.dot(
        hidden.T,
        lax.all_gather(cot_mean, "zero", axis=1, tiled=True),
        preferred_element_type=jnp.float32,
    )
    owned = lax.psum_scatter(
        terms.astype(jnp.bfloat16), "dp", scatter_dimension=1, tiled=True
    ).astype(jnp.float32)
    label_wide = label_rows.astype(jnp.float32)
    grad_true = (
        owned - jnp.dot(label_total[:, :cands], label_wide, precision=lax.Precision.HIGHEST)
    ) * factor
    grad_sampled = (
        owned - jnp.dot(label_total[:, cands:], label_wide, precision=lax.Precision.HIGHEST)
    ) * factor
    low_bits = bits % 128
    high_bits = bits // 128
    noise_one = (low_bits.astype(jnp.float32) + 0.5) / 128.0
    noise_two = (high_bits.astype(jnp.float32) + 0.5) / 128.0
    noise_three = (((3 * low_bits + 5 * high_bits) % 128).astype(jnp.float32) + 0.5) / 128.0
    new_moment = dither(
        beta_one * moment.astype(jnp.float32) + (1.0 - beta_one) * grad_true, noise_one
    )
    new_curvature = dither(
        beta_two * curvature.astype(jnp.float32) + (1.0 - beta_two) * grad_sampled * grad_sampled,
        noise_two,
    )
    ratio = jnp.clip(
        new_moment.astype(jnp.float32) / (gamma_rate * new_curvature.astype(jnp.float32)), -1.0, 1.0
    )
    shrunk = weight.astype(jnp.float32) * (1.0 - learn_rate * decay_rate) - learn_rate * ratio
    weight_piece = dither(shrunk, noise_three)
    new_weight = lax.all_gather(weight_piece, "dp", axis=1, tiled=True)
    return (new_weight, new_moment, new_curvature)


def solution(mesh):
    in_specs = (
        P(None, "dp", "zero"),
        P("dp", "zero"),
        P(None, "dp"),
        P("dp"),
        P("dp"),
        P("zero", "dp"),
        P("zero", "dp"),
        P("zero", "dp"),
        P("zero", "dp"),
    )
    out_specs = (P("zero", None), P("zero", "dp"), P("zero", "dp"))
    return jax.shard_map(
        on_device, mesh=mesh, in_specs=in_specs, out_specs=out_specs, check_vma=False
    )
```

profile of v0, /device:TPU:4, one launch (start us, length us, event | category | flops | bytes accessed | tf_op | source)
XLA Modules:
  0.0 387.3 jit_solution(16972792300468119694)
XLA Ops:
  8.0 0.0 copy-start
  8.0 0.0 all-gather.3.cloned.1.call-start
  8.1 0.7 all-gather.3.cloned.1.call-update
  8.7 0.0 all-reduce.2.cloned.1.call-start
  8.8 0.8 iota_compare_fusion
  9.6 1.2 fusion.17
  10.8 0.9 convolution_convert_fusion.1
  11.8 0.0 all-reduce.2.cloned.1.call-update
  11.8 0.0 copy-start.1
  11.8 0.0 copy-start.2
  11.8 0.0 reduce-scatter.2.cloned.1.call-start
  11.9 99.6 %all-gather.3.cloned.1.call-done = bf16[256,4096]{1,0:T(8,128)(2,1)} async-done(((bf16[256,128]{1,0:T(8,128)(2,1)}), bf16[256,4096]{1,0:T(8,128)(2,1)}) %all-gather.3.cloned.1.call-update) | async-done | bytes 2097168 | tf_op jit(solution)/shard_map/all_gather | solution.py:39
  111.4 4.6 %convolution_convert_fusion = bf16[448,4096]{1,0:T(8,128)(2,1)} fusion(bf16[256,448]{0,1:T(8,128)(2,1)S(1)} %fusion.17, bf16[256,4096]{1,0:T(8,128)(2,1)} %all-gather.3.cloned.1.call-done), kind=kOutput, calls=%fused_computation | convolution fusion | flops 941359104 | bytes 5996544 | tf_op jit(solution)/shard_map/dot_general | solution.py:37
  116.0 0.0 copy-start.3
  116.0 0.0 copy-start.4
  116.0 0.0 reduce-scatter.2.cloned.1.call-update
  116.0 0.0 all-gather.5.cloned.1.call-start
  116.1 67.2 %all-reduce.2.cloned.1.call-done = bf16[448,128]{1,0:T(8,128)(2,1)} async-done(((bf16[448,128]{1,0:T(8,128)(2,1)}), bf16[448,128]{1,0:T(8,128)(2,1)}) %all-reduce.2.cloned.1.call-update) | async-done | bytes 114704 | tf_op jit(solution)/shard_map/psum | solution.py:36
  183.2 96.9 %reduce-scatter.2.cloned.1.call-done = bf16[448,256]{1,0:T(8,128)(2,1)} async-done(((bf16[448,4096]{1,0:T(8,128)(2,1)}), bf16[448,256]{1,0:T(8,128)(2,1)}) %reduce-scatter.2.cloned.1.call-update) | async-done | bytes 229392 | tf_op jit(solution)/shard_map/reduce_scatter | solution.py:42
  280.2 0.0 copy-done
  280.2 0.0 copy-done.1
  280.2 0.0 copy-done.2
  280.2 1.4 fusion.3
  281.6 0.0 copy-done.3
  281.6 0.0 copy-done.4
  281.6 0.0 copy-start.5
  281.7 3.0 fusion.16
  284.7 0.0 copy-done.5
  284.7 0.0 all-gather.5.cloned.1.call-update
  284.7 90.7 %all-gather.5.cloned.1.call-done = bf16[448,4096]{1,0:T(8,128)(2,1)} async-done(((bf16[448,256]{1,0:T(8,128)(2,1)}), bf16[448,4096]{1,0:T(8,128)(2,1)}) %all-gather.5.cloned.1.call-update) | async-done | bytes 3670032 | tf_op jit(solution)/shard_map/all_gather | solution.py:69
  375.4 4.3 %copy.18 = bf16[448,4096]{1,0:T(8,128)(2,1)} copy(bf16[448,4096]{1,0:T(8,128)(2,1)} %all-gather.5.cloned.1.call-done) | data formatting | bytes 7340032
Async XLA Ops:
  8.0 272.2 %copy-start = (bf16[64,256]{1,0:T(8,128)(2,1)S(1)}, bf16[64,256]{1,0:T(8,128)(2,1)}, u32[]{:S(2)}) copy-start(bf16[64,256]{1,0:T(8,128)(2,1)} %param.11) | copy-start | bytes 98308
  8.0 103.4 %all-gather.3.cloned.1.call-start = ((), (), s32[]{:S(2)}) async-start(), calls=%async_computation.1 | async-start | bytes 2162688 | tf_op jit(solution)/shard_map/all_gather | solution.py:39
  8.7 174.5 %all-reduce.2.cloned.1.call-start = ((), (), s32[]{:S(2)}) async-start(), calls=%async_computation.3 | async-start | bytes 229376 | tf_op jit(solution)/shard_map/psum | solution.py:36
  11.8 268.4 %copy-start.1 = (s32[448,256]{1,0:T(8,128)S(1)}, s32[448,256]{1,0:T(8,128)}, u32[]{:S(2)}) copy-start(s32[448,256]{1,0:T(8,128)} %param.17) | copy-start | bytes 1376260
  11.8 268.4 %copy-start.2 = (bf16[448,256]{1,0:T(8,128)(2,1)S(1)}, bf16[448,256]{1,0:T(8,128)(2,1)}, u32[]{:S(2)}) copy-start(bf16[448,256]{1,0:T(8,128)(2,1)} %param.15) | copy-start | bytes 688132
  11.8 268.3 %reduce-scatter.2.cloned.1.call-start = ((), (), s32[]{:S(2)}) async-start(), calls=%async_computation.2 | async-start | bytes 3899392 | tf_op jit(solution)/shard_map/reduce_scatter | solution.py:42
  116.0 165.6 %copy-start.3 = (bf16[448,256]{1,0:T(8,128)(2,1)S(1)}, bf16[448,256]{1,0:T(8,128)(2,1)}, u32[]{:S(2)}) copy-start(bf16[448,256]{1,0:T(8,128)(2,1)} %param.14) | copy-start | bytes 688132
  116.0 165.6 %copy-start.4 = (bf16[448,256]{1,0:T(8,128)(2,1)S(1)}, bf16[448,256]{1,0:T(8,128)(2,1)}, u32[]{:S(2)}) copy-start(bf16[448,256]{1,0:T(8,128)(2,1)} %param.16) | copy-start | bytes 688132
  116.0 259.4 %all-gather.5.cloned.1.call-start = ((), (), s32[]{:S(2)}) async-start(), calls=%async_computation.4 | async-start | bytes 3899392 | tf_op jit(solution)/shard_map/all_gather | solution.py:69
  281.6 3.1 copy-start.5
Sparse Core Ops, SparseCore 0:
  12.5 98.9 all-gather.2
Sparse Core Ops, SparseCore 1:
  12.7 170.5 all-reduce.1
  186.8 93.3 reduce-scatter.1
  284.8 90.5 all-gather.4
where the time goes:
time: 388 us; the launch traced here: 387 us
  waiting for transfers between devices  355 us (91%)
  between operations  15.7 us (4%)
  matrix products  9.97 us (3%)
  local copies, waits for them, and re-layouts  4.33 us (1%)
    all_gather x1, waiting for transfers between devices, on_device(): lax.all_gather(cot_mean, 'zero', axis=1, tiled=True)  99.6 us
    reduce_scatter x1, waiting for transfers between devices, on_device(): lax.psum_scatter(terms.astype(jnp.bfloat16), 'dp', scatter_dimension=1, t...  96.9 us
    all_gather x1, waiting for transfers between devices, on_device(): new_weight = lax.all_gather(weight_piece, 'dp', axis=1, tiled=True)  90.7 us
    psum x1, waiting for transfers between devices, on_device(): lax.psum(label_part.astype(jnp.bfloat16), 'dp').astype(jnp.float32)  67.2 us
  transfers between devices with their start and end apart: 4, of which 4 were waited for; matrix products, arithmetic and copies ran while one was open for 2% of the time, Pallas kernels for 0%

commit v1 on v0

--- a/solution.py
+++ b/solution.py
@@ -9,6 +9,13 @@
 gamma_rate = 0.5
 learn_rate = 0.05
 decay_rate = 0.1
+
+
+def swapped_in(x, axis, d):
+    n_dev = lax.axis_size(axis)
+    shards = jnp.stack([x for _ in range(n_dev)])
+    shards = lax.all_to_all(shards, axis, split_axis=0, concat_axis=0)
+    return jnp.concatenate(shards, axis=d)
 
 
 def dither(value, noise):
@@ -34,11 +41,7 @@
         preferred_element_type=jnp.float32,
     )
     label_total = lax.psum(label_part.astype(jnp.bfloat16), "dp").astype(jnp.float32)
-    terms = jnp.dot(
-        hidden.T,
-        lax.all_gather(cot_mean, "zero", axis=1, tiled=True),
-        preferred_element_type=jnp.float32,
-    )
+    terms = jnp.dot(hidden.T, swapped_in(cot_mean, "zero", 1), preferred_element_type=jnp.float32)
     owned = lax.psum_scatter(
         terms.astype(jnp.bfloat16), "dp", scatter_dimension=1, tiled=True
     ).astype(jnp.float32)

time: 388 us -> 417 us (1.075)
  waiting for transfers between devices: 355 us -> 372 us
  starting transfers between devices: 0.17 us -> 16.1 us
    all_gather x1 -> x0, waiting for transfers between devices: 99.6 us -> none  [on_device(): lax.all_gather(cot_mean, 'zero', axis=1, tiled=True)]
    psum x1, waiting for transfers between devices: 67.2 us -> 129 us  [on_device(): lax.psum(label_part.astype(jnp.bfloat16), 'dp').astype(jnp.float32)]
    all_to_all x0 -> x1, waiting for transfers between devices: none -> 53.9 us  [swapped_in(): shards = lax.all_to_all(shards, axis, split_axis=0, concat_axis=0)]
    all_to_all x0 -> x1, starting transfers between devices: none -> 15.9 us  [swapped_in(): shards = lax.all_to_all(shards, axis, split_axis=0, concat_axis=0)]
  transfers between devices with their start and end apart: 4 -> 4, of which waited for: 4 -> 4; matrix products, arithmetic and copies ran while one was open for 2% -> 1% of each run, Pallas kernels for 0% -> 0%
where the time goes in v1:
time: 417 us
  waiting for transfers between devices  372 us (89%)
  starting transfers between devices  16.1 us (4%)
  between operations  13.9 us (3%)
  matrix products  8.46 us (2%)
  local copies, waits for them, and re-layouts  6.89 us (2%)
    psum x1, waiting for transfers between devices, on_device(): lax.psum(label_part.astype(jnp.bfloat16), 'dp').astype(jnp.float32)  129 us
    reduce_scatter x1, waiting for transfers between devices, on_device(): lax.psum_scatter(terms.astype(jnp.bfloat16), 'dp', scatter_dimension=1, t...  97 us
    all_gather x1, waiting for transfers between devices, on_device(): new_weight = lax.all_gather(weight_piece, 'dp', axis=1, tiled=True)  91.2 us
    all_to_all x1, waiting for transfers between devices, swapped_in(): shards = lax.all_to_all(shards, axis, split_axis=0, concat_axis=0)  53.9 us
    all_to_all x1, starting transfers between devices, swapped_in(): shards = lax.all_to_all(shards, axis, split_axis=0, concat_axis=0)  15.9 us
  transfers between devices with their start and end apart: 4, of which 4 were waited for; matrix products, arithmetic and copies ran while one was open for 1% of the time, Pallas kernels for 0%

profile of v1, /device:TPU:4, one launch (start us, length us, event | category | flops | bytes accessed | tf_op | source)
XLA Modules:
  0.0 417.1 jit_solution(14103303800977296007)
XLA Ops:
  7.2 0.0 copy-start
  7.2 0.0 copy-start.1
  7.2 0.0 copy-start.2
  7.2 0.0 copy-start.3
  7.2 1.0 copy.12
  8.2 1.6 stack.2
  9.8 15.9 %all-to-all-start = ((bf16[32,256,128]{1,2,0:T(8,128)(2,1)}), bf16[32,256,128]{1,2,0:T(8,128)(2,1)S(1)}, u32[]{:S(2)}, u32[]{:S(2)}) async-start(bf16[32,256,128]{1,2,0:T(8,128)(2,1)} %stack.2), calls=%async_computation | async-start | bytes 4194304 | tf_op jit(solution)/shard_map/all_to_all | solution.py:17
  25.7 0.0 all-reduce.2.cloned.1.call-start
  25.8 0.0 copy-done.1
  25.8 0.0 copy-done.2
  25.8 0.1 iota_compare_fusion
  25.9 0.0 copy-done.3
  25.9 1.0 convolution_convert_fusion.1
  26.9 0.0 all-reduce.2.cloned.1.call-update
  26.9 0.0 reduce-scatter.2.cloned.1.call-start
  27.0 53.9 %all-to-all-done = bf16[32,256,128]{1,2,0:T(8,128)(2,1)S(1)} async-done(((bf16[32,256,128]{1,2,0:T(8,128)(2,1)}), bf16[32,256,128]{1,2,0:T(8,128)(2,1)S(1)}, u32[]{:S(2)}, u32[]{:S(2)}) %all-to-all-start) | async-done | bytes 2097184 | tf_op jit(solution)/shard_map/all_to_all | solution.py:17
  80.9 3.0 convolution_convert_fusion
  83.9 0.0 copy-start.4
  83.9 0.0 copy-start.5
  83.9 0.0 copy-start.6
  83.9 0.0 copy-start.7
  83.9 0.0 reduce-scatter.2.cloned.1.call-update
  84.0 0.0 all-gather.2.cloned.1.call-start
  84.0 129.4 %all-reduce.2.cloned.1.call-done = bf16[448,128]{1,0:T(8,128)(2,1)} async-done(((bf16[448,128]{1,0:T(8,128)(2,1)}), bf16[448,128]{1,0:T(8,128)(2,1)}) %all-reduce.2.cloned.1.call-update) | async-done | bytes 114704 | tf_op jit(solution)/shard_map/psum | solution.py:43
  213.4 97.0 %reduce-scatter.2.cloned.1.call-done = bf16[448,256]{1,0:T(8,128)(2,1)} async-done(((bf16[448,4096]{1,0:T(8,128)(2,1)}), bf16[448,256]{1,0:T(8,128)(2,1)}) %reduce-scatter.2.cloned.1.call-update) | async-done | bytes 229392 | tf_op jit(solution)/shard_map/reduce_scatter | solution.py:45
  310.5 0.0 copy-done
  310.5 0.0 copy-done.4
  310.5 0.0 copy-done.5
  310.5 1.4 fusion.3
  311.9 0.0 copy-done.6
  311.9 0.0 copy-done.7
  311.9 0.0 copy-start.8
  312.0 3.0 fusion.23
  315.0 0.0 copy-done.8
  315.0 0.0 all-gather.2.cloned.1.call-update
  315.0 91.2 %all-gather.2.cloned.1.call-done = bf16[448,4096]{1,0:T(8,128)(2,1)} async-done(((bf16[448,256]{1,0:T(8,128)(2,1)}), bf16[448,4096]{1,0:T(8,128)(2,1)}) %all-gather.2.cloned.1.call-update) | async-done | bytes 3670032 | tf_op jit(solution)/shard_map/all_gather | solution.py:72
  406.2 4.3 %copy.19 = bf16[448,4096]{1,0:T(8,128)(2,1)} copy(bf16[448,4096]{1,0:T(8,128)(2,1)} %all-gather.2.cloned.1.call-done) | data formatting | bytes 7340032
Async XLA Ops:
  7.2 303.3 %copy-start = (bf16[64,256]{1,0:T(8,128)(2,1)S(1)}, bf16[64,256]{1,0:T(8,128)(2,1)}, u32[]{:S(2)}) copy-start(bf16[64,256]{1,0:T(8,128)(2,1)} %param.11) | copy-start | bytes 98308
  7.2 18.6 %copy-start.1 = (s32[256]{0:T(256)S(1)}, s32[256]{0:T(256)}, u32[]{:S(2)}) copy-start(s32[256]{0:T(256)} %param.13) | copy-start | bytes 3076
  7.2 18.6 %copy-start.2 = (s32[256]{0:T(256)S(1)}, s32[256]{0:T(256)}, u32[]{:S(2)}) copy-start(s32[256]{0:T(256)} %param.12) | copy-start | bytes 3076
  7.2 18.7 %copy-start.3 = (bf16[2,256,448]{1,2,0:T(8,128)(2,1)S(1)}, bf16[2,256,448]{1,2,0:T(8,128)(2,1)}, u32[]{:S(2)}) copy-start(bf16[2,256,448]{1,2,0:T(8,128)(2,1)} %param.9) | copy-start | bytes 1376260
  9.8 71.2 %all-to-all-start = ((bf16[32,256,128]{1,2,0:T(8,128)(2,1)}), bf16[32,256,128]{1,2,0:T(8,128)(2,1)S(1)}, u32[]{:S(2)}, u32[]{:S(2)}) async-start(bf16[32,256,128]{1,2,0:T(8,128)(2,1)} %stack.2), calls=%async_computation | async-start | bytes 4194304 | tf_op jit(solution)/shard_map/all_to_all | solution.py:17
  25.7 187.7 %all-reduce.2.cloned.1.call-start = ((), (), s32[]{:S(2)}) async-start(), calls=%async_computation.3 | async-start | bytes 229376 | tf_op jit(solution)/shard_map/psum | solution.py:43
  26.9 283.5 %reduce-scatter.2.cloned.1.call-start = ((), (), s32[]{:S(2)}) async-start(), calls=%async_computation.2 | async-start | bytes 3899392 | tf_op jit(solution)/shard_map/reduce_scatter | solution.py:45
  83.9 226.5 %copy-start.4 = (s32[448,256]{1,0:T(8,128)S(1)}, s32[448,256]{1,0:T(8,128)}, u32[]{:S(2)}) copy-start(s32[448,256]{1,0:T(8,128)} %param.17) | copy-start | bytes 1376260
  83.9 226.6 %copy-start.5 = (bf16[448,256]{1,0:T(8,128)(2,1)S(1)}, bf16[448,256]{1,0:T(8,128)(2,1)}, u32[]{:S(2)}) copy-start(bf16[448,256]{1,0:T(8,128)(2,1)} %param.15) | copy-start | bytes 688132
  83.9 228.0 %copy-start.6 = (bf16[448,256]{1,0:T(8,128)(2,1)S(1)}, bf16[448,256]{1,0:T(8,128)(2,1)}, u32[]{:S(2)}) copy-start(bf16[448,256]{1,0:T(8,128)(2,1)} %param.14) | copy-start | bytes 688132
  83.9 228.0 %copy-start.7 = (bf16[448,256]{1,0:T(8,128)(2,1)S(1)}, bf16[448,256]{1,0:T(8,128)(2,1)}, u32[]{:S(2)}) copy-start(bf16[448,256]{1,0:T(8,128)(2,1)} %param.16) | copy-start | bytes 688132
  84.0 322.3 %all-gather.2.cloned.1.call-start = ((), (), s32[]{:S(2)}) async-start(), calls=%async_computation.4 | async-start | bytes 3899392 | tf_op jit(solution)/shard_map/all_gather | solution.py:72
  311.9 3.1 copy-start.8
Sparse Core Ops, SparseCore 0:
  30.0 183.3 all-reduce.1
  217.1 93.3 reduce-scatter.1
  315.1 91.0 all-gather.1
